TPU v7x, 32 devices: a whole 2x2x4 slice. The times are simulated.
32 devices in a mesh: seq: 8 (over z, x), head: 4 (over y, core).
Axes of the slice: x: 2, y: 2, z: 4, core: 2. Of those that a mesh axis runs over, the one named last changes fastest.
Arguments:
- queries: bfloat16 [2048, 4096], P('seq', 'head'), may hold values from -8 to 8
- suffix_key_value: bfloat16 [2048, 2, 2048], P('seq', None, 'head'), may hold values from -8 to 8
- pooled_pages: bfloat16 [128, 256, 2, 2048], P('seq', None, None, 'head'), may hold values from -8 to 8
- out_weight: bfloat16 [4096, 5376], P('head'), may hold values from -0.5 to 0.5
- page_table: int32 [4, 32], replicated, may hold values from 0 to 127, as said below
- prefix_len: int32 [4], replicated, may hold values from 1024 to 8192, as said below
- suffix_len: int32 [4], replicated, may hold values from 2 to 512, as said below
Outputs:
- projected: bfloat16 [2048, 5376], P('seq', 'head')
Inputs may be any that keep to these rules, and one draw needn't show every extreme that they name: `page_table`: every slot of the pool appears exactly once; slot s lies on index s // 16 of seq, and every index of seq holds exactly 4 pages of every request. `prefix_len`: some request has exactly 8192 prefix tokens. `suffix_len`: some request has exactly 512 live suffix tokens.
All inputs are finite; a program needn't handle non-finite values.
Results may differ from a plain program's by a relative error of at most 0.013.
Values may be sent and summed in bfloat16 or wider, within the bound.
No kernel may reach another device: no remote copies, remote signals or barrier semaphores. Data moves between devices by JAX's collectives and lax.ppermute only.
A program may use at most 192 MiB of HBM per device.

v0:
```python
import jax
import jax.numpy as jnp
from jax import lax
from jax.sharding import PartitionSpec as P

D = 5376
QUERY_HEADS = 32
KEY_VALUE_HEADS = 16
HEAD_WIDTH = 128


def shifted(x, axis, by):
    devices = lax.axis_size(axis)
    pairs = [(i, i + by) for i in range(devices) if 0 <= i + by < devices]
    return lax.ppermute(x, axis, pairs)


def page_ranks(page_table, pages_dev):
    owners = page_table // pages_dev
    earlier = (owners[:, :, None] == owners[:, None, :]) & (
        page_table[:, None, :] < page_table[:, :, None]
    )
    return (owners, jnp.sum(earlier.astype(jnp.int32), axis=2))


def pack_pages(pooled_pages, kept_pages, slot_of, local_slot, slot_width):
    columns = jnp.arange(slot_width, dtype=jnp.int32)
    matched = kept_pages[:, None, :] & (slot_of[:, None, :] == columns[None, :, None])
    chosen_slot = jnp.sum(jnp.where(matched, local_slot[:, None, :], 0), axis=2).reshape(-1)
    filled = jnp.any(matched, axis=2).reshape(-1)
    chosen = jnp.take(pooled_pages, chosen_slot, axis=0)
    return jnp.where(filled[:, None, None, None], chosen, jnp.zeros_like(chosen))


def page_mask(my_owners, slot_of, wanted, seq_count, slot_width, rows_of_pages, my_prefix):
    sources = jnp.arange(seq_count, dtype=jnp.int32)
    columns = jnp.arange(slot_width, dtype=jnp.int32)
    matched = (
        wanted[:, None, :]
        & (my_owners[None, None, :] == sources[:, None, None])
        & (slot_of[None, None, :] == columns[None, :, None])
    )
    page_index = jnp.arange(my_owners.shape[0], dtype=jnp.int32)
    first_row = jnp.sum(jnp.where(matched, page_index[None, None, :], 0), axis=2) * rows_of_pages
    filled = jnp.any(matched, axis=2)
    offsets = jnp.arange(rows_of_pages, dtype=jnp.int32)
    positions = first_row[:, :, None] + offsets[None, None, :]
    return (filled[:, :, None] & (positions < my_prefix)).reshape(1, -1)


def attend(query_head, key_parts, score_scale):
    tok_rows = query_head.shape[0]
    group_of_heads = query_head.shape[1]
    head_size = query_head.shape[2]
    flat_query = query_head.reshape(tok_rows * group_of_heads, head_size)
    score_list = []
    row_max = None
    for key_rows, value_rows, visible in key_parts:
        scores = jnp.einsum("qd,spd->qsp", flat_query, key_rows, preferred_element_type=jnp.float32)
        scores = scores.reshape(tok_rows, group_of_heads, -1) * score_scale
        part_max = jnp.max(jnp.where(visible[:, None, :], scores, -jnp.inf), axis=2)
        row_max = part_max if row_max is None else jnp.maximum(row_max, part_max)
        score_list.append(scores)
    row_total = jnp.zeros((tok_rows, group_of_heads), jnp.float32)
    mixed_sum = jnp.zeros((tok_rows, group_of_heads, head_size), jnp.float32)
    for (key_rows, value_rows, visible), scores in zip(key_parts, score_list):
        weights = jnp.where(visible[:, None, :], jnp.exp(scores - row_max[:, :, None]), 0.0)
        row_total = row_total + jnp.sum(weights, axis=2)
        rounded = weights.astype(jnp.bfloat16).reshape(
            tok_rows * group_of_heads, value_rows.shape[0], value_rows.shape[1]
        )
        product = jnp.einsum("qsp,spd->qd", rounded, value_rows, preferred_element_type=jnp.float32)
        mixed_sum = mixed_sum + product.reshape(tok_rows, group_of_heads, head_size)
    return mixed_sum / row_total[:, :, None]


def shards(queries, suffix_key_value, pooled_pages, out_weight, page_table, prefix_len, suffix_len):
    tok_rows = queries.shape[0]
    pages_dev = pooled_pages.shape[0]
    rows_of_pages = pooled_pages.shape[1]
    kv_local = suffix_key_value.shape[2] // HEAD_WIDTH
    group_of_heads = QUERY_HEADS // KEY_VALUE_HEADS
    score_scale = float(D // QUERY_HEADS) ** (-0.5)
    seq_count = lax.axis_size("seq")
    half_count = seq_count // 2
    seq_index = lax.axis_index("seq")
    member = seq_index // half_count
    request = seq_index % half_count
    holding = 2 * pages_dev // seq_count
    owners, rank_table = page_ranks(page_table, pages_dev)
    picked = jnp.arange(page_table.shape[0], dtype=jnp.int32) == request
    my_prefix = jnp.sum(jnp.where(picked, prefix_len, 0))
    my_suffix = jnp.sum(jnp.where(picked, suffix_len, 0))
    my_owners = jnp.sum(jnp.where(picked[:, None], owners, 0), axis=0)
    my_ranks = jnp.sum(jnp.where(picked[:, None], rank_table, 0), axis=0)
    send_owners = jnp.concatenate([owners, owners], axis=0)
    send_ranks = jnp.concatenate([rank_table, rank_table], axis=0)
    slot_table = page_table % pages_dev
    send_slots = jnp.concatenate([slot_table, slot_table], axis=0)
    held_here = send_owners == seq_index
    previous = shifted(suffix_key_value, "seq", half_count)
    suffix_rows = jnp.concatenate([previous, suffix_key_value], axis=0)
    query_pos = member * tok_rows + jnp.arange(tok_rows, dtype=jnp.int32)
    key_index = jnp.arange(2 * tok_rows, dtype=jnp.int32)
    own_pos = member * tok_rows + key_index - tok_rows
    earlier_part = (key_index < tok_rows) & (member == 1) & (key_index < my_suffix)
    later_part = (key_index >= tok_rows) & (own_pos < my_suffix)
    suffix_visible = earlier_part[None, :] | later_part[None, :] & (
        own_pos[None, :] <= query_pos[:, None]
    )
    outgoing = pack_pages(pooled_pages, held_here, send_ranks, send_slots, holding)
    received = lax.all_to_all(outgoing, "seq", split_axis=0, concat_axis=0, tiled=True)
    all_sources = jnp.ones((seq_count, my_owners.shape[0]), dtype=jnp.bool_)
    page_parts = [
        (
            received,
            page_mask(
                my_owners, my_ranks, all_sources, seq_count, holding, rows_of_pages, my_prefix
            ),
        )
    ]
    query_layout = queries.reshape(tok_rows, kv_local, group_of_heads, HEAD_WIDTH)
    heads_out = []
    for head_slot in range(kv_local):
        head_start = head_slot * HEAD_WIDTH
        head_stop = head_start + HEAD_WIDTH
        key_parts = [
            (
                page_block[:, :, 0, head_start:head_stop],
                page_block[:, :, 1, head_start:head_stop],
                visible,
            )
            for page_block, visible in page_parts
        ]
        key_parts.append(
            (
                suffix_rows[None, :, 0, head_start:head_stop],
                suffix_rows[None, :, 1, head_start:head_stop],
                suffix_visible,
            )
        )
        heads_out.append(attend(query_layout[:, head_slot], key_parts, score_scale))
    attention = jnp.stack(heads_out, axis=1)
    live_query = (query_pos < my_suffix)[:, None, None, None]
    attention = jnp.where(live_query, attention, 0.0).astype(jnp.bfloat16).reshape(tok_rows, -1)
    partial_value = jnp.dot(attention, out_weight, preferred_element_type=jnp.float32)
    summed = lax.psum_scatter(
        partial_value.astype(jnp.bfloat16), "head", scatter_dimension=1, tiled=True
    )
    return summed


def solution(mesh):
    placed = (
        P("seq", "head"),
        P("seq", None, "head"),
        P("seq", None, None, "head"),
        P("head", None),
        P(),
        P(),
        P(),
    )
    return jax.shard_map(
        shards, mesh=mesh, in_specs=placed, out_specs=P("seq", "head"), check_vma=False
    )
```

profile of v0, /device:TPU:0, one launch (start us, length us, event | category | flops | bytes accessed | tf_op | source)
XLA Modules:
  0.0 743.0 jit_solution(11335090849496143313)
XLA Ops:
  6.5 0.7 add_select_fusion
  7.2 1.0 convert_reduce_fusion
  8.2 0.1 fusion.73
  8.4 0.2 select_reduce_fusion.12
  9.0 38.2 %gather_fusion = bf16[32,256,2,512]{3,2,1,0:T(2,128)(2,1)} fusion(bf16[16,256,2,512]{3,2,1,0:T(2,128)(2,1)} %param.9, s32[1024]{0:T(1024)S(1)} %pad_clamp_fusion), kind=kCustom, calls=%fused_computation | custom fusion | bytes 33554560 | tf_op jit(solution)/shard_map/jit(_take)/gather | solution.py:31
  47.2 20.2 %broadcast_select_fusion.1 = bf16[32,256,2,512]{3,2,1,0:T(2,128)(2,1)S(1)} fusion(pred[32]{0:T(512)(128)(4,1)S(1)} %broadcast_in_dim.213, bf16[32,256,2,512]{3,2,1,0:T(2,128)(2,1)} %gather_fusion, pred[32]{0:T(512)(128)(4,1)S(1)} %compare_and_fusion), kind=kLoop, calls=%fused_computation.2 | loop fusion | flops 16777216 | bytes 33554496 | tf_op jit(solution)/shard_map/jit(_where)/select_n | solution.py:32
  67.5 7.5 %copy.120 = bf16[32,256,2,512]{3,1,2,0:T(8,128)(2,1)} copy(bf16[32,256,2,512]{3,2,1,0:T(2,128)(2,1)S(1)} %broadcast_select_fusion.1) | data formatting | bytes 33554432 | tf_op jit(solution)/shard_map/jit(_where)/select_n | solution.py:32
  75.0 7.4 all-to-all-start
  82.5 5.9 collective-permute-start
  88.5 0.2 and_reduce_fusion
  88.9 0.2 fusion.71
  89.2 0.2 copy.122
  89.6 0.8 copy.137
  90.6 0.7 select_reduce_fusion.15
  91.4 0.6 fusion.77
  92.0 1.1 broadcast_compare_fusion.1
  93.1 0.8 fusion.70
  93.9 0.6 fusion.76
  94.5 0.8 fusion.69
  95.3 0.3 and_or_fusion
  95.5 269.2 %collective-permute-done = bf16[256,2,512]{2,0,1:T(8,128)(2,1)} collective-permute-done((bf16[256,2,512]{2,0,1:T(8,128)(2,1)S(1)}, bf16[256,2,512]{2,0,1:T(8,128)(2,1)}, u32[]{:S(2)}, u32[]{:S(2)}) %collective-permute-start) | collective-permute-done | bytes 524320 | tf_op jit(solution)/shard_map/ppermute | solution.py:15
  364.8 1.1 constant_dynamic-update-slice_fusion.1
  365.9 1.3 select_reduce_fusion.11
  367.2 0.1 copy.127
  367.4 0.1 reduce_max.90
  367.5 0.3 fusion.16
  367.8 1.2 fusion.17
  369.0 76.5 %all-to-all-done = bf16[32,256,2,512]{3,1,2,0:T(8,128)(2,1)} async-done(((bf16[32,256,2,512]{3,1,2,0:T(8,128)(2,1)}), bf16[32,256,2,512]{3,1,2,0:T(8,128)(2,1)}, u32[]{:S(2)}, u32[]{:S(2)}) %all-to-all-start) | async-done | bytes 16777248 | tf_op jit(solution)/shard_map/all_to_all | solution.py:112
  445.5 7.8 %select_reduce_fusion.7 = (f32[512]{0:T(512)S(1)}, f32[32,256,512]{2,1,0:T(8,128)}) fusion(pred[32,256]{1,0:T(8,128)(4,1)S(1)} %fusion.70, bf16[512,128,1]{1,0,2:T(8,128)(2,1)S(1)} %bitcast.200, bf16[32,256,2,512]{3,1,2,0:T(8,128)(2,1)} %all-to-all-done), kind=kOutput, calls=%fused_computation.22 | convolution fusion | flops 1086324224 | bytes 19015680 | tf_op jit(solution)/shard_map/qd,spd->qsp/dot_general | solution.py:59
  453.3 0.1 reduce_max.91
  453.5 0.6 max.40
  454.1 3.5 fusion.41
  457.6 0.1 copy.138
  457.8 0.7 reduce_max.94
  458.5 0.1 copy.149
  458.6 0.7 reduce_max.98
  459.5 0.7 reduce_max.102
  460.2 4.0 fusion.13
  464.3 11.3 %fusion.12 = f32[32,256,512]{2,1,0:T(8,128)} fusion(bf16[512,128,1]{1,0,2:T(8,128)(2,1)S(1)} %bitcast.199, bf16[32,256,2,512]{3,1,2,0:T(8,128)(2,1)} %all-to-all-done), kind=kOutput, calls=%fused_computation.34 | convolution fusion | flops 1073741824 | bytes 19005440 | tf_op jit(solution)/shard_map/qd,spd->qsp/dot_general | solution.py:59
  475.6 19.7 %select_reduce_fusion.6 = (f32[512]{0:T(512)S(1)}, f32[512]{0:T(512)S(1)}, f32[512]{0:T(512)S(1)}, f32[512]{0:T(512)S(1)}, f32[32,256,512]{2,1,0:T(8,128)}) fusion(f32[32,256,512]{2,1,0:T(8,128)} %get-tuple-element.32, f32[512]{0:T(512)S(1)} %copy-done.11, pred[32,256]{1,0:T(8,128)(4,1)S(1)} %fusion.70, f32[32,256,512]{2,1,0:T(8,128)S(1)} %fusion.13, ...), kind=kOutput, calls=%fused_computation.20 | convolution fusion | flops 1128265728 | bytes 69355520 | tf_op jit(solution)/shard_map/qd,spd->qsp/dot_general | solution.py:59
  495.3 0.1 reduce_max.103
  495.5 0.1 reduce_max.99
  495.6 0.1 reduce_max.95
  495.8 18.7 %select_reduce_fusion.4 = (f32[512]{0:T(512)S(1)}, f32[512]{0:T(512)S(1)}, f32[512]{0:T(512)S(1)}) fusion(f32[32,256,512]{2,1,0:T(8,128)} %get-tuple-element.35, f32[512]{0:T(512)S(1)} %max.42, pred[32,256]{1,0:T(8,128)(4,1)S(1)} %fusion.70, f32[512]{0:T(512)S(1)} %max.44, f32[32,256,512]{2,1,0:T(8,128)} %copy-done, f32[512]{0:T(512)S(1)} %max.46, ...), kind=kLoop, calls=%fused_computation.17 | loop fusion | flops 50330112 | bytes 50352128 | tf_op jit(solution)/shard_map/reduce_sum | solution.py:68
  514.5 33.8 %fusion.3 = (bf16[512,256,32]{0,1,2:T(8,128)(2,1)}, bf16[512,256,32]{0,1,2:T(8,128)(2,1)}, bf16[512,256,32]{0,1,2:T(8,128)(2,1)}, bf16[512,256,32]{0,1,2:T(8,128)(2,1)}) fusion(f32[32,256,512]{2,1,0:T(8,128)} %get-tuple-element.32, f32[512]{0:T(512)S(1)} %copy-done.11, pred[256,32]{0,1:T(8,128)(4,1)S(1)} %fusion.69, f32[512]{0:T(512)S(1)} %max.42, ...), kind=kLoop, calls=%fused_computation.10 | loop fusion | flops 67108864 | bytes 100679680 | tf_op jit(solution)/shard_map/convert_element_type | solution.py:69
  548.4 14.6 %copy.128 = bf16[512,256,32]{1,2,0:T(8,128)(2,1)} copy(bf16[512,256,32]{0,1,2:T(8,128)(2,1)} %get-tuple-element.25) | data formatting | bytes 16777216 | tf_op jit(solution)/shard_map/convert_element_type | solution.py:69
  563.0 0.1 reduce_sum.154
  563.3 0.1 reduce_sum.151
  563.5 0.1 reduce_sum.157
  563.8 0.1 reduce_sum.160
  564.2 14.6 %copy.139 = bf16[512,256,32]{1,2,0:T(8,128)(2,1)} copy(bf16[512,256,32]{0,1,2:T(8,128)(2,1)} %get-tuple-element.26) | data formatting | bytes 16777216 | tf_op jit(solution)/shard_map/convert_element_type | solution.py:69
  578.8 14.6 %copy.150 = bf16[512,256,32]{1,2,0:T(8,128)(2,1)} copy(bf16[512,256,32]{0,1,2:T(8,128)(2,1)} %get-tuple-element.27) | data formatting | bytes 16777216 | tf_op jit(solution)/shard_map/convert_element_type | solution.py:69
  593.4 14.8 %copy.161 = bf16[512,256,32]{1,2,0:T(8,128)(2,1)} copy(bf16[512,256,32]{0,1,2:T(8,128)(2,1)} %get-tuple-element.28) | data formatting | bytes 16777216 | tf_op jit(solution)/shard_map/convert_element_type | solution.py:69
  608.3 13.2 %fusion.28 = f32[256,2,128]{0,2,1:T(8,128)S(1)} fusion(bf16[32,256,2,512]{3,1,2,0:T(8,128)(2,1)} %all-to-all-done, bf16[256,2,256,32]{2,3,1,0:T(8,128)(2,1)} %bitcast.185), kind=kOutput, calls=%fused_computation.64 | convolution fusion | flops 1073741824 | bytes 10747904 | tf_op jit(solution)/shard_map/qsp,spd->qd/dot_general | solution.py:72
  621.4 1.6 fusion.21
  623.0 2.0 fusion.43
  625.1 13.4 %fusion.31 = f32[256,2,128]{0,2,1:T(8,128)S(1)} fusion(bf16[32,256,2,512]{3,1,2,0:T(8,128)(2,1)} %all-to-all-done, bf16[256,2,256,32]{2,3,1,0:T(8,128)(2,1)} %bitcast.192), kind=kOutput, calls=%fused_computation.65 | convolution fusion | flops 1073741824 | bytes 10747904 | tf_op jit(solution)/shard_map/qsp,spd->qd/dot_general | solution.py:72
  638.5 1.4 fusion.23
  639.9 11.0 %fusion.34 = f32[256,2,128]{0,2,1:T(8,128)S(1)} fusion(bf16[32,256,2,512]{3,1,2,0:T(8,128)(2,1)} %all-to-all-done, bf16[256,2,256,32]{2,3,1,0:T(8,128)(2,1)S(1)} %bitcast.191), kind=kOutput, calls=%fused_computation.66 | convolution fusion | flops 1073741824 | bytes 10747904 | tf_op jit(solution)/shard_map/qsp,spd->qd/dot_general | solution.py:72
  650.9 1.2 fusion.25
  652.2 10.7 %fusion.37 = f32[256,2,128]{0,2,1:T(8,128)S(1)} fusion(bf16[32,256,2,512]{3,1,2,0:T(8,128)(2,1)} %all-to-all-done, bf16[256,2,256,32]{2,3,1,0:T(8,128)(2,1)S(1)} %bitcast.188), kind=kOutput, calls=%fused_computation.67 | convolution fusion | flops 1073741824 | bytes 10747904 | tf_op jit(solution)/shard_map/qsp,spd->qd/dot_general | solution.py:72
  662.9 1.2 fusion.27
  664.4 10.2 %convolution_convert_fusion = bf16[256,5376]{0,1:T(8,128)(2,1)} fusion(bf16[256,1024]{0,1:T(8,128)(2,1)S(1)} %fusion.40, bf16[1024,5376]{1,0:T(8,128)(2,1)} %param.10), kind=kOutput, calls=%fused_computation.31 | convolution fusion | flops 2819948544 | bytes 14286848 | tf_op jit(solution)/shard_map/dot_general | solution.py:146
  674.6 61.3 %reduce-scatter.2.cloned.1.call-done = bf16[256,1344]{0,1:T(8,128)(2,1)} async-done(((bf16[256,5376]{0,1:T(8,128)(2,1)}), bf16[256,1344]{0,1:T(8,128)(2,1)}) %reduce-scatter.2.cloned.1.call-update) | async-done | bytes 688144 | tf_op jit(solution)/shard_map/reduce_scatter | solution.py:147
  (97 shorter events, 2.6 us)
Async XLA Ops:
  75.0 7.5 %copy-start.2 = (bf16[256,2,512]{2,1,0:T(2,128)(2,1)S(1)}, bf16[256,2,512]{2,1,0:T(2,128)(2,1)}, u32[]{:S(2)}) copy-start(bf16[256,2,512]{2,1,0:T(2,128)(2,1)} %param.8) | copy-start | bytes 1572868
  75.0 14.2 %copy-start.4 = (bf16[256,1024]{1,0:T(8,128)(2,1)S(1)}, bf16[256,1024]{1,0:T(8,128)(2,1)}, u32[]{:S(2)}) copy-start(bf16[256,1024]{1,0:T(8,128)(2,1)} %param.7) | copy-start | bytes 1572868
  75.0 15.6 %copy-start.16 = (s32[4]{0:T(128)S(1)}, s32[4]{0:T(128)}, u32[]{:S(2)}) copy-start(s32[4]{0:T(128)} %param.12) | copy-start | bytes 52
  75.0 15.6 %copy-start.17 = (s32[4]{0:T(128)S(1)}, s32[4]{0:T(128)}, u32[]{:S(2)}) copy-start(s32[4]{0:T(128)} %param.13) | copy-start | bytes 52
  75.0 370.5 %all-to-all-start = ((bf16[32,256,2,512]{3,1,2,0:T(8,128)(2,1)}), bf16[32,256,2,512]{3,1,2,0:T(8,128)(2,1)}, u32[]{:S(2)}, u32[]{:S(2)}) async-start(bf16[32,256,2,512]{3,1,2,0:T(8,128)(2,1)} %copy.120), calls=%async_computation | async-start | bytes 33554432 | tf_op jit(solution)/shard_map/all_to_all | solution.py:112
  82.4 653.5 %reduce-scatter.2.cloned.1.call-start = ((), (), s32[]{:S(2)}) async-start(), calls=%async_computation.2 | async-start | bytes 3440640 | tf_op jit(solution)/shard_map/reduce_scatter | solution.py:147
  82.5 282.2 %collective-permute-start = (bf16[256,2,512]{2,0,1:T(8,128)(2,1)S(1)}, bf16[256,2,512]{2,0,1:T(8,128)(2,1)}, u32[]{:S(2)}, u32[]{:S(2)}) collective-permute-start(bf16[256,2,512]{2,0,1:T(8,128)(2,1)S(1)} %copy.125), channel_id=1, source_target_pairs={{0,16},{4,20},{8,24},{12,28},{1,17},{5,21},{9,25},{13,29},{2,18},{... | collective-permute-start | bytes 1572872 | tf_op jit(solution)/shard_map/ppermute | solution.py:15
  365.9 1.6 copy-start.3
  454.1 6.1 copy-start.8
  457.6 2.6 copy-start.6
  460.2 15.3 %copy-start.5 = (bf16[256,1,2,128]{3,2,0,1:T(2,128)(2,1)S(1)}, bf16[256,1,2,128]{3,2,0,1:T(2,128)(2,1)}, u32[]{:S(2)}) copy-start(bf16[256,1,2,128]{3,2,0,1:T(2,128)(2,1)} %copy.137) | copy-start | bytes 393220
  464.3 31.0 %copy-start = (f32[32,256,512]{2,1,0:T(8,128)}, f32[32,256,512]{2,1,0:T(8,128)S(1)}, u32[]{:S(2)}) copy-start(f32[32,256,512]{2,1,0:T(8,128)S(1)} %fusion.13) | copy-start | bytes 50331652
  464.3 11.3 %copy-start.11 = (f32[512]{0:T(512)S(1)}, f32[512]{0:T(512)}, u32[]{:S(2)}) copy-start(f32[512]{0:T(512)} %max.40) | copy-start | bytes 6148
  475.6 19.9 %copy-start.14 = (f32[512]{0:T(512)S(1)}, f32[512]{0:T(512)}, u32[]{:S(2)}) copy-start(f32[512]{0:T(512)} %reduce_max.102) | copy-start | bytes 6148
  475.6 20.0 %copy-start.13 = (f32[512]{0:T(512)S(1)}, f32[512]{0:T(512)}, u32[]{:S(2)}) copy-start(f32[512]{0:T(512)} %reduce_max.98) | copy-start | bytes 6148
  475.6 20.2 %copy-start.12 = (f32[512]{0:T(512)S(1)}, f32[512]{0:T(512)}, u32[]{:S(2)}) copy-start(f32[512]{0:T(512)} %reduce_max.94) | copy-start | bytes 6148
  548.4 14.9 %copy-start.7 = (f32[256,2]{0,1:T(2,128)S(1)}, f32[256,2]{0,1:T(2,128)}, u32[]{:S(2)}) copy-start(f32[256,2]{0,1:T(2,128)} %copy-done.6) | copy-start | bytes 6148
  578.8 29.4 %copy-start.10 = (f32[256,2]{0,1:T(2,128)S(1)}, f32[256,2]{0,1:T(2,128)}, u32[]{:S(2)}) copy-start(f32[256,2]{0,1:T(2,128)} %get-tuple-element.5) | copy-start | bytes 6148
  593.4 28.0 %copy-start.9 = (f32[256,2]{0,1:T(2,128)S(1)}, f32[256,2]{0,1:T(2,128)}, u32[]{:S(2)}) copy-start(f32[256,2]{0,1:T(2,128)} %copy-done.8) | copy-start | bytes 6148
  608.2 30.2 %copy-start.1 = (f32[256,2,512]{0,2,1:T(8,128)S(1)}, f32[256,2,512]{0,2,1:T(8,128)}, u32[]{:S(2)}) copy-start(f32[256,2,512]{0,2,1:T(8,128)} %get-tuple-element.36) | copy-start | bytes 3145732
  608.3 31.6 %slice-start.2 = ((s8[8388608]{0:T(1024)(128)(4,1)}), s8[4194304]{0:T(1024)(128)(4,1)S(1)}, s32[]{:S(2)}) async-start(s8[8388608]{0:T(1024)(128)(4,1)} %bitcast.189), calls=%async_computation.5 | async-start | bytes 8388608
  623.0 16.8 %slice-start.3 = ((s8[8388608]{0:T(1024)(128)(4,1)}), s8[4194304]{0:T(1024)(128)(4,1)S(1)}, s32[]{:S(2)}) async-start(s8[8388608]{0:T(1024)(128)(4,1)} %bitcast.189), calls=%async_computation.6 | async-start | bytes 8388608
  625.0 27.1 %slice-start = ((s8[8388608]{0:T(1024)(128)(4,1)}), s8[4194304]{0:T(1024)(128)(4,1)S(1)}, s32[]{:S(2)}) async-start(s8[8388608]{0:T(1024)(128)(4,1)} %bitcast.186), calls=%async_computation.3 | async-start | bytes 8388608
  638.4 13.7 %slice-start.1 = ((s8[8388608]{0:T(1024)(128)(4,1)}), s8[4194304]{0:T(1024)(128)(4,1)S(1)}, s32[]{:S(2)}) async-start(s8[8388608]{0:T(1024)(128)(4,1)} %bitcast.186), calls=%async_computation.4 | async-start | bytes 8388608
  639.9 24.4 %copy-start.15 = (pred[256]{0:T(512)(128)(4,1)S(1)}, pred[256]{0:T(512)(128)(4,1)}, u32[]{:S(2)}) copy-start(pred[256]{0:T(512)(128)(4,1)} %broadcast_compare_fusion.1) | copy-start | bytes 772
Sparse Core Ops, SparseCore 0:
  674.8 61.1 reduce-scatter.1
where the time goes:
time: 748 us; the launch traced here: 743 us
  waiting for transfers between devices  407 us (54%)
  matrix products  113 us (15%)
  local copies, waits for them, and re-layouts  112 us (15%)
  other arithmetic  83 us (11%)
  between operations  14.3 us (2%)
  starting transfers between devices  13.3 us (2%)
    ppermute x1, waiting for transfers between devices, shifted(): return lax.ppermute(x, axis, pairs)  269 us
    all_to_all x1, waiting for transfers between devices, shards(): lax.all_to_all(outgoing, 'seq', split_axis=0, concat_axis=0, tiled=True)  76.5 us
    reduce_scatter x1, waiting for transfers between devices, shards(): lax.psum_scatter(partial_value.astype(jnp.bfloat16), 'head', scatter_dime...  61.3 us
    convert_element_type x4, local copies, waits for them, and re-layouts, attend(): weights.astype(jnp.bfloat16)  58.7 us
    dot_general x8, matrix products, attend(): jnp.einsum('qsp,spd->qd', rounded, value_rows, preferred_element_type=jnp...  53.7 us
    dot_general x8, matrix products, attend(): jnp.einsum('qd,spd->qsp', flat_query, key_rows, preferred_element_type=jn...  49 us
    gather x1, local copies, waits for them, and re-layouts, pack_pages(): chosen = jnp.take(pooled_pages, chosen_slot, axis=0)  38.2 us
    convert_element_type x1, other arithmetic, attend(): weights.astype(jnp.bfloat16)  33.8 us
  transfers between devices with their start and end apart: 3, of which 3 were waited for; matrix products, arithmetic and copies ran while one was open for 2% of the time, Pallas kernels for 0%

commit v1 on v0

v1 whole, which is shorter than its diff:
```python
import functools
import math

import jax
import jax.numpy as jnp
from jax import lax
from jax.experimental import pallas as pl
from jax.experimental.pallas import tpu as pltpu
from jax.sharding import PartitionSpec as P

D = 5376
QUERY_HEADS = 32
KEY_VALUE_HEADS = 16
HEAD_WIDTH = 128
GROUP = QUERY_HEADS // KEY_VALUE_HEADS
RATE = float(D // QUERY_HEADS) ** (-0.5) * math.log2(math.e)
HIDDEN = -(2.0**99)
STAT = 128
SUM_HIGH = 32
SUM_LOW = 64
F32 = jnp.float32
BF16 = jnp.bfloat16
MIB = 1 << 20


def ring_member(place, count):
    return jnp.where(place < count // 2, 2 * place, 2 * (count - 1 - place) + 1)


def ring_place(member, count):
    return jnp.where(member % 2 == 0, member // 2, count - 1 - member // 2)


def ring_order(count):
    return list(range(0, count, 2)) + list(range(count - 1, 0, -2))


def same_request_at(offset, count):
    order = ring_order(count)
    half = count // 2
    return any(order[(i + offset) % count] % half == order[i] % half for i in range(count))


def tables(page_table, prefix_len, suffix_len, pages_dev, holding, page_rows, seq_index, count):
    mine = page_table // pages_dev == seq_index
    index = jnp.arange(page_table.shape[1], dtype=jnp.int32)
    before = mine[:, None, :] & (index[None, None, :] < index[None, :, None])
    rank = jnp.sum(before.astype(jnp.int32), axis=2)
    wanted = jnp.arange(holding, dtype=jnp.int32)
    pick = mine[:, None, :] & (rank[:, None, :] == wanted[None, :, None])
    slots = jnp.sum(jnp.where(pick, (page_table % pages_dev)[:, None, :], 0), axis=2)
    first = jnp.sum(jnp.where(pick, index[None, None, :] * page_rows, 0), axis=2)
    valid = jnp.clip(prefix_len[:, None] - first, 0, page_rows)
    live = jnp.sum((valid > 0).astype(jnp.int32), axis=1)
    place = ring_place(seq_index, count)
    here = jnp.stack([place, seq_index]).astype(jnp.int32)
    return jnp.concatenate([slots.reshape(-1), valid.reshape(-1), live, suffix_len, here])


class Meta:
    def __init__(self, count, holding):
        self.count = count
        self.half = count // 2
        self.holding = holding
        self.valid_at = self.half * holding
        self.live_at = 2 * self.half * holding
        self.suffix_at = self.live_at + self.half
        self.place_at = self.suffix_at + self.half

    def chunk(self, meta, offset):
        place = (meta[self.place_at] + (offset + self.count)) % self.count
        return ring_member(place, self.count)

    def slot(self, meta, request, page):
        return meta[request * self.holding + page]

    def valid(self, meta, request, page):
        return meta[self.valid_at + request * self.holding + page]


def attend_kernel(info, offset, row_base, tok_rows, with_suffix, meta, q_ref, *refs):
    holding = info.holding
    k_refs = refs[:holding]
    v_refs = refs[holding : 2 * holding]
    sk_ref, sv_ref = refs[2 * holding : 2 * holding + 2]
    blocks = len(refs) - (2 * holding + 2) - 3
    out_refs = refs[2 * holding + 2 : 2 * holding + 2 + blocks]
    acc_ref, max_ref, sum_ref = refs[-3:]
    group = pl.program_id(0)
    block = pl.program_id(1)
    rows = q_ref.shape[0]
    keys = k_refs[0].shape[1]
    chunk = info.chunk(meta, offset)
    request = chunk % info.half
    member = chunk // info.half
    suffix = meta[info.suffix_at + request]
    first = member * tok_rows + row_base + block * rows
    live_rows = suffix > first
    live_pages = meta[info.live_at + request]
    width = HEAD_WIDTH

    def stacked():
        return jnp.concatenate(
            [q_ref[:, i * width : (i + 1) * width] for i in range(GROUP)], axis=0
        )

    def scores_of(query, keys_block):
        return lax.dot_general(
            query, keys_block, (((1,), (1,)), ((), ())), preferred_element_type=F32
        )

    max_ref[...] = jnp.full(max_ref.shape, HIDDEN, F32)
    sum_ref[...] = jnp.zeros(sum_ref.shape, F32)
    acc_ref[...] = jnp.zeros(acc_ref.shape, F32)

    for pages in range(1, holding + 1):

        @pl.when(live_rows & (live_pages == pages))
        def _(pages=pages):
            query = stacked()
            parts = [scores_of(query, k_refs[j][0]) for j in range(pages)]
            column = lax.broadcasted_iota(jnp.int32, parts[-1].shape, 1)
            limit = info.valid(meta, request, pages - 1)
            parts[-1] = jnp.where(column < limit, parts[-1], HIDDEN)
            top = parts[0]
            for part in parts[1:]:
                top = jnp.maximum(top, part)
            row_max = jnp.max(top, axis=1, keepdims=True).astype(BF16).astype(F32)
            total = None
            mixed = None
            for j in range(pages):
                weight = jnp.exp2((parts[j] - row_max) * RATE)
                total = weight if total is None else total + weight
                product = jnp.dot(weight.astype(BF16), v_refs[j][0], preferred_element_type=F32)
                mixed = product if mixed is None else mixed + product
            max_ref[...] = row_max
            sum_ref[...] = jnp.sum(total, axis=1, keepdims=True)
            acc_ref[...] = mixed

    if with_suffix:
        seq_index = meta[info.place_at + 1]
        here = seq_index // info.half
        sees = (request == seq_index % info.half) & (member >= here)

        @pl.when(live_rows & sees)
        def _():
            scores = scores_of(stacked(), sk_ref[...])
            key = here * tok_rows + lax.broadcasted_iota(jnp.int32, scores.shape, 1)
            row = lax.broadcasted_iota(jnp.int32, scores.shape, 0) % rows
            visible = (key < suffix) & (key <= first + row)
            scores = jnp.where(visible, scores, HIDDEN)
            old_max = max_ref[...]
            row_max = jnp.max(scores, axis=1, keepdims=True).astype(BF16).astype(F32)
            row_max = jnp.maximum(row_max, old_max)
            weight = jnp.where(visible, jnp.exp2((scores - row_max) * RATE), 0.0)
            keep = jnp.exp2((old_max - row_max) * RATE)
            product = jnp.dot(weight.astype(BF16), sv_ref[...], preferred_element_type=F32)
            max_ref[...] = row_max
            sum_ref[...] = sum_ref[...] * keep + jnp.sum(weight, axis=1, keepdims=True)
            acc_ref[...] = acc_ref[...] * keep + product

    stat_at = out_refs[0].shape[1] - STAT
    lane = lax.broadcasted_iota(jnp.int32, (rows, STAT), 1)
    for number, out_ref in enumerate(out_refs):

        @pl.when(block == number)
        def _(out_ref=out_ref):
            @pl.when(group == 0)
            def _():
                out_ref[:, stat_at:] = jnp.zeros((rows, STAT), BF16)

            stats = out_ref[:, stat_at:].astype(F32)
            for i in range(GROUP):
                part = slice(i * rows, (i + 1) * rows)
                head = group * GROUP + i
                column = pl.multiple_of(head * width, width)
                out_ref[:, pl.ds(column, width)] = acc_ref[part, :].astype(BF16)
                total = sum_ref[part, :]
                high = total.astype(BF16).astype(F32)
                stats = jnp.where(lane == head, max_ref[part, :], stats)
                stats = jnp.where(lane == SUM_HIGH + head, high, stats)
                stats = jnp.where(lane == SUM_LOW + head, total - high, stats)
            out_ref[:, stat_at:] = stats.astype(BF16)


def attend(info, meta, query, offset, row_base, tok_rows, key_pages, value_pages, suffix_keys, suffix_values):
    rows = min(128, query.shape[0])
    blocks = query.shape[0] // rows
    columns = query.shape[1]
    holding = info.holding
    kv_local = key_pages.shape[2] // HEAD_WIDTH
    page_rows = key_pages.shape[1]
    wide = GROUP * HEAD_WIDTH

    def page_map(page, group, block, meta):
        request = info.chunk(meta, offset) % info.half
        return (info.slot(meta, request, page), 0, group)

    page_specs = [
        pl.BlockSpec((1, page_rows, HEAD_WIDTH), functools.partial(page_map, j))
        for j in range(holding)
    ]
    suffix_spec = pl.BlockSpec((tok_rows, HEAD_WIDTH), lambda g, t, meta: (0, g))
    out_spec = pl.BlockSpec((rows, columns + STAT), lambda g, t, meta: (0, 0))
    out = jax.ShapeDtypeStruct((rows, columns + STAT), BF16)
    work = query.shape[0] * kv_local * GROUP * holding * page_rows
    return pl.pallas_call(
        functools.partial(
            attend_kernel, info, offset, row_base, tok_rows, same_request_at(offset, info.count)
        ),
        grid_spec=pltpu.PrefetchScalarGridSpec(
            num_scalar_prefetch=1,
            grid=(kv_local, blocks),
            in_specs=[pl.BlockSpec((rows, wide), lambda g, t, meta: (t, g))]
            + page_specs
            + page_specs
            + [suffix_spec, suffix_spec],
            out_specs=[out_spec] * blocks,
            scratch_shapes=[
                pltpu.VMEM((GROUP * rows, HEAD_WIDTH), F32),
                pltpu.VMEM((GROUP * rows, 1), F32),
                pltpu.VMEM((GROUP * rows, 1), F32),
            ],
        ),
        out_shape=[out] * blocks,
        compiler_params=pltpu.CompilerParams(vmem_limit_bytes=24 * MIB),
        cost_estimate=pl.CostEstimate(
            flops=4 * work * HEAD_WIDTH,
            bytes_accessed=2 * query.size * 2 + 4 * holding * page_rows * kv_local * HEAD_WIDTH,
            transcendentals=work,
        ),
        name="attend",
    )(meta, query, *([key_pages] * holding), *([value_pages] * holding), suffix_keys, suffix_values)


def combine(packed):
    stat_at = packed[0].shape[1] - STAT
    stats = [one[:, stat_at:].astype(F32) for one in packed]
    top = stats[0]
    for one in stats[1:]:
        top = jnp.maximum(top, one)
    factors = [jnp.exp2((jnp.minimum(one - top, 0.0)) * RATE) for one in stats]
    total = None
    for one, factor in zip(stats, factors):
        own = pltpu.roll(one, STAT - SUM_HIGH, 1) + pltpu.roll(one, STAT - SUM_LOW, 1)
        total = own * factor if total is None else total + own * factor
    heads = []
    for head in range(stat_at // HEAD_WIDTH):
        mixed = None
        for one, factor in zip(packed, factors):
            value = one[:, head * HEAD_WIDTH : (head + 1) * HEAD_WIDTH].astype(F32)
            value = value * factor[:, head : head + 1]
            mixed = value if mixed is None else mixed + value
        heads.append(mixed)
    return (heads, top, total)


def merge_kernel(a_ref, b_ref, out_ref):
    heads, top, total = combine([a_ref[...], b_ref[...]])
    for head, mixed in enumerate(heads):
        out_ref[:, head * HEAD_WIDTH : (head + 1) * HEAD_WIDTH] = mixed.astype(BF16)
    high = total.astype(BF16).astype(F32)
    lane = lax.broadcasted_iota(jnp.int32, top.shape, 1)
    stats = jnp.where(lane < SUM_HIGH, top, 0.0)
    stats = jnp.where((lane >= SUM_HIGH) & (lane < SUM_LOW), pltpu.roll(high, SUM_HIGH, 1), stats)
    low = pltpu.roll(total - high, SUM_LOW, 1)
    stats = jnp.where((lane >= SUM_LOW) & (lane < SUM_LOW + SUM_HIGH), low, stats)
    out_ref[:, len(heads) * HEAD_WIDTH :] = stats.astype(BF16)


def merge(a, b):
    return pl.pallas_call(
        merge_kernel,
        out_shape=jax.ShapeDtypeStruct(a.shape, BF16),
        in_specs=[pl.BlockSpec(memory_space=pltpu.VMEM)] * 2,
        out_specs=pl.BlockSpec(memory_space=pltpu.VMEM),
        compiler_params=pltpu.CompilerParams(vmem_limit_bytes=16 * MIB),
        cost_estimate=pl.CostEstimate(
            flops=6 * a.size, bytes_accessed=6 * a.size, transcendentals=0
        ),
        name="merge",
    )(a, b)


def finish_kernel(info, tok_rows, blocks, meta, target, *refs):
    packed = refs[: 3 * blocks]
    w_ref, give_ref, keep_ref, attention = refs[3 * blocks :]
    step = pl.program_id(0)
    half_steps = pl.num_programs(0) // 2
    rows = packed[0].shape[0]

    @pl.when(step == 0)
    def _():
        chunk = info.chunk(meta, 0)
        suffix = meta[info.suffix_at + chunk % info.half]
        for block in range(blocks):
            heads, _, total = combine([ref[...] for ref in packed[3 * block : 3 * block + 3]])
            first = (chunk // info.half) * tok_rows + block * rows
            place = first + lax.broadcasted_iota(jnp.int32, heads[0].shape, 0)
            for head, mixed in enumerate(heads):
                value = jnp.where(place < suffix, mixed / total[:, head : head + 1], 0.0)
                attention[
                    block * rows : (block + 1) * rows,
                    head * HEAD_WIDTH : (head + 1) * HEAD_WIDTH,
                ] = value.astype(BF16)

    product = jnp.dot(attention[...], w_ref[0], preferred_element_type=F32).astype(BF16)

    @pl.when(step < half_steps)
    def _():
        give_ref[0] = product

    @pl.when(step >= half_steps)
    def _():
        keep_ref[0] = product


def finish(info, meta, targets, packed, weight, tok_rows):
    blocks = len(packed) // 3
    count, depth, columns = weight.shape
    half = count // 2
    whole = pl.BlockSpec(packed[0].shape, lambda i, meta, target: (0, 0))
    out = jax.ShapeDtypeStruct((half, tok_rows, columns), BF16)
    return pl.pallas_call(
        functools.partial(finish_kernel, info, tok_rows, blocks),
        grid_spec=pltpu.PrefetchScalarGridSpec(
            num_scalar_prefetch=2,
            grid=(count,),
            in_specs=[whole] * len(packed)
            + [pl.BlockSpec((1, depth, columns), lambda i, meta, target: (target[i], 0, 0))],
            out_specs=[
                pl.BlockSpec(
                    (1, tok_rows, columns),
                    lambda i, meta, target: (jnp.minimum(i, half - 1), 0, 0),
                ),
                pl.BlockSpec(
                    (1, tok_rows, columns),
                    lambda i, meta, target: (jnp.maximum(i - half, 0), 0, 0),
                ),
            ],
            scratch_shapes=[pltpu.VMEM((tok_rows, depth), BF16)],
        ),
        out_shape=[out, out],
        compiler_params=pltpu.CompilerParams(vmem_limit_bytes=40 * MIB),
        cost_estimate=pl.CostEstimate(
            flops=2 * tok_rows * depth * columns * count,
            bytes_accessed=2 * weight.size,
            transcendentals=0,
        ),
        name="finish",
    )(meta, targets, *packed, weight)


def shards(queries, suffix_key_value, pooled_pages, out_weight, page_table, prefix_len, suffix_len):
    tok_rows = queries.shape[0]
    pages_dev, page_rows = pooled_pages.shape[:2]
    count = lax.axis_size("seq")
    reach = count // 2
    seq_index = lax.axis_index("seq")
    holding = 2 * pages_dev // count
    info = Meta(count, holding)
    order = ring_order(count)
    ahead = [(order[i], order[(i + 1) % count]) for i in range(count)]
    back = [(b, a) for a, b in ahead]

    middle = tok_rows // 2
    from_left = [queries]
    from_right = [queries]
    for step in range(1, reach):
        from_left.append(lax.ppermute(from_left[-1], "seq", ahead))
        from_right.append(lax.ppermute(from_right[-1], "seq", back))
    from_left.append(lax.ppermute(from_left[-1][:middle], "seq", ahead))
    from_right.append(lax.ppermute(from_right[-1][middle:], "seq", back))

    meta = tables(
        page_table, prefix_len, suffix_len, pages_dev, holding, page_rows, seq_index, count
    )
    keys = (
        pooled_pages[:, :, 0, :],
        pooled_pages[:, :, 1, :],
        suffix_key_value[:, 0, :],
        suffix_key_value[:, 1, :],
    )
    head_count = lax.axis_size("head")
    columns = out_weight.shape[1] // head_count
    weight = jnp.swapaxes(out_weight.reshape(-1, head_count, columns), 0, 1)

    home = attend(info, meta, queries, 0, 0, tok_rows, *keys)
    left = [home]
    right = [home]
    for step in range(1, reach):
        left.append(attend(info, meta, from_left[step], -step, 0, tok_rows, *keys))
        right.append(attend(info, meta, from_right[step], step, 0, tok_rows, *keys))
    left.append(attend(info, meta, from_left[reach], -reach, 0, tok_rows, *keys))
    right.append(attend(info, meta, from_right[reach], reach, middle, tok_rows, *keys))

    low_left = lax.ppermute(left[reach][0], "seq", back)
    high_right = lax.ppermute(right[reach][0], "seq", ahead)
    high_left = None
    low_right = None
    for step in range(reach - 1, 0, -1):
        low_left = lax.ppermute(merge(low_left, left[step][0]), "seq", back)
        high_right = lax.ppermute(merge(high_right, right[step][1]), "seq", ahead)
        mine_left = left[step][1] if high_left is None else merge(high_left, left[step][1])
        high_left = lax.ppermute(mine_left, "seq", back)
        mine_right = right[step][0] if low_right is None else merge(low_right, right[step][0])
        low_right = lax.ppermute(mine_right, "seq", ahead)

    head_index = lax.axis_index("head")
    half = head_count // 2
    pair = head_index // 2
    core = head_index % 2
    turn = (pair + jnp.arange(half, dtype=jnp.int32)) % half
    targets = jnp.concatenate([2 * turn + 1 - core, 2 * turn + core])
    packed = [home[0], low_left, low_right, home[1], high_left, high_right]
    give, keep = finish(info, meta, targets, packed, weight, tok_rows)
    taken = lax.ppermute(give, "head", [(i, i ^ 1) for i in range(head_count)])
    total = keep.astype(F32) + taken.astype(F32)
    result = total[0]
    for step in range(1, half):
        pairs = [(i, (i + 2 * step) % head_count) for i in range(head_count)]
        result = result + lax.ppermute(total[step].astype(BF16), "head", pairs).astype(F32)
    return result.astype(BF16)


def solution(mesh):
    placed = (
        P("seq", "head"),
        P("seq", None, "head"),
        P("seq", None, None, "head"),
        P("head", None),
        P(),
        P(),
        P(),
    )
    return jax.shard_map(
        shards, mesh=mesh, in_specs=placed, out_specs=P("seq", "head"), check_vma=False
    )
```

time: 748 us -> 240 us (0.32)
  waiting for transfers between devices: 407 us -> 40.7 us
  matrix products: 113 us -> 0 us
  other arithmetic: 83 us -> 3.3 us
  Pallas kernels: 0 us -> 78.4 us
  local copies, waits for them, and re-layouts: 112 us -> 77.9 us
  starting transfers between devices: 13.3 us -> 34.9 us
  between operations: 14.3 us -> 0.4 us
    ppermute x1 -> x24, waiting for transfers between devices: 269 us -> 40.7 us  [the longest x3 18.2 us: shards(): from_right.append(lax.ppermute(from_right[-1], 'seq', back))]
    dot_general x17 -> x0, matrix products: 113 us -> none  [the longest x8 53.7 us: attend(): jnp.einsum('qsp,spd->qd', rounded, value_rows, preferred_element_type=jnp...]
    pallas_call x0 -> x20, Pallas kernels: none -> 78.4 us  [the longest x9 63.3 us: attend(): pl.pallas_call(functools.partial(attend_kernel, info, offset, row_base, t...]
    all_to_all x1 -> x0, waiting for transfers between devices: 76.5 us -> none  [shards(): lax.all_to_all(outgoing, 'seq', split_axis=0, concat_axis=0, tiled=True)]
    reduce_scatter x1 -> x0, waiting for transfers between devices: 61.3 us -> none  [shards(): lax.psum_scatter(partial_value.astype(jnp.bfloat16), 'head', scatter_dime...]
    convert_element_type x4, local copies, waits for them, and re-layouts: 58.7 us -> 7.98 us  [the longest x2 3.3 us: shards(): total[step].astype(BF16)]
    gather x1 -> x0, local copies, waits for them, and re-layouts: 38.2 us -> none  [pack_pages(): chosen = jnp.take(pooled_pages, chosen_slot, axis=0)]
    convert_element_type x2 -> x1, other arithmetic: 33.9 us -> 2.35 us  [shards(): return result.astype(BF16)]
  transfers between devices with their start and end apart: 3 -> 24, of which waited for: 3 -> 5; matrix products, arithmetic and copies ran while one was open for 2% -> 24% of each run, Pallas kernels for 0% -> 29%
where the time goes in v1:
time: 240 us; the launch traced here: 236 us
  Pallas kernels  78.4 us (33%)
  local copies, waits for them, and re-layouts  77.9 us (32%)
  waiting for transfers between devices  40.7 us (17%)
  starting transfers between devices  34.9 us (15%)
  other arithmetic  3.3 us (1%)
    pallas_call x9, Pallas kernels, attend(): pl.pallas_call(functools.partial(attend_kernel, info, offset, row_base, t...  63.3 us
    unnamed x29, local copies, waits for them, and re-layouts  25 us
    ppermute x3, waiting for transfers between devices, shards(): from_right.append(lax.ppermute(from_right[-1], 'seq', back))  18.2 us
    ppermute x1, waiting for transfers between devices, shards(): lax.ppermute(total[step].astype(BF16), 'head', pairs).astype(F32)  16.3 us
    slice x1, local copies, waits for them, and re-layouts, shards(): pooled_pages[:, :, 1, :]  16.2 us
    reshape x1, local copies, waits for them, and re-layouts, shards(): weight = jnp.swapaxes(out_weight.reshape(-1, head_count, columns), 0, 1)  15.2 us
    pallas_call x1, Pallas kernels, finish(): pl.pallas_call(functools.partial(finish_kernel, info, tok_rows, blocks),...  9.38 us
    ppermute x3, starting transfers between devices, shards(): high_left = lax.ppermute(mine_left, 'seq', back)  7.55 us
  transfers between devices with their start and end apart: 24, of which 5 were waited for; matrix products, arithmetic and copies ran while one was open for 24% of the time, Pallas kernels for 29%

profile of v1, /device:TPU:0, one launch (start us, length us, event | category | flops | bytes accessed | tf_op | source)
XLA Modules:
  0.0 235.6 jit_solution(2464374037558494657)
XLA Ops:
  0.0 2.9 %collective-permute-start.8 = (bf16[256,1024]{1,0:T(8,128)(2,1)}, bf16[256,1024]{1,0:T(8,128)(2,1)S(1)}, u32[]{:S(2)}, u32[]{:S(2)}) collective-permute-start(bf16[256,1024]{1,0:T(8,128)(2,1)} %q_ref.1), channel_id=1, source_target_pairs={{8,0},{16,8},{24,16},{28,24},{20,28},{12,20},{4,12},{0,4},{9,1},{1... | collective-permute-start | bytes 1572872 | tf_op jit(solution)/shard_map/ppermute | solution.py:371
  3.0 16.2 %fusion.8 = (bf16[16,256,1,512]{3,2,1,0:T(2,128)(2,1)S(1)}, bf16[16,256,1,512]{3,2,1,0:T(2,128)(2,1)S(1)}) fusion(bf16[16,256,2,512]{3,2,1,0:T(2,128)(2,1)} %param.9), kind=kLoop, calls=%fused_computation.36 | loop fusion | bytes 16777216 | tf_op jit(solution)/shard_map/slice | solution.py:380
  19.3 4.8 %copy_bitcast_fusion = (bf16[16,256,512]{2,1,0:T(8,128)(2,1)}, bf16[16,256,512]{2,1,0:T(8,128)(2,1)}) fusion(bf16[16,256,1,512]{3,2,1,0:T(2,128)(2,1)S(1)} %get-tuple-element.41, bf16[16,256,1,512]{3,2,1,0:T(2,128)(2,1)S(1)} %get-tuple-element.42), kind=kLoop, calls=%fused_computation | loop fusion | bytes 16777216 | tf_op jit(solution)/shard_map/squeeze | solution.py:380
  24.1 1.9 collective-permute-start.9
  26.2 11.3 %collective-permute-done.9.q_ref = bf16[256,1024]{1,0:T(8,128)(2,1)S(1)} collective-permute-done((bf16[256,1024]{1,0:T(8,128)(2,1)S(1)}, bf16[256,1024]{1,0:T(8,128)(2,1)S(1)}, u32[]{:S(2)}, u32[]{:S(2)}) %collective-permute-start.9) | collective-permute-done | bytes 524320 | tf_op jit(solution)/shard_map/ppermute | solution.py:371
  37.5 1.7 collective-permute-start.10
  39.3 0.4 collective-permute-start.2
  39.7 0.2 select_reduce_fusion
  40.0 3.1 %fusion.9 = (bf16[256,1,512]{2,1,0:T(2,128)(2,1)}, bf16[256,1,512]{2,1,0:T(2,128)(2,1)}) fusion(bf16[256,2,512]{2,1,0:T(2,128)(2,1)} %param.8), kind=kLoop, calls=%fused_computation.37 | loop fusion | bytes 1048576 | tf_op jit(solution)/shard_map/slice | solution.py:382
  43.0 6.9 %collective-permute-done.10.q_ref = bf16[256,1024]{1,0:T(8,128)(2,1)S(1)} collective-permute-done((bf16[256,1024]{1,0:T(8,128)(2,1)S(1)}, bf16[256,1024]{1,0:T(8,128)(2,1)S(1)}, u32[]{:S(2)}, u32[]{:S(2)}) %collective-permute-start.10) | collective-permute-done | bytes 524320 | tf_op jit(solution)/shard_map/ppermute | solution.py:371
  50.0 0.7 slice.34
  50.7 1.4 collective-permute-start.17
  52.0 0.2 convert_reduce_fusion.1
  52.5 0.7 collective-permute-start.3
  53.2 1.3 copy_bitcast_fusion.2
  54.6 2.7 %collective-permute-done.17.q_ref = bf16[128,1024]{1,0:T(8,128)(2,1)S(1)} collective-permute-done((bf16[128,1024]{1,0:T(8,128)(2,1)}, bf16[128,1024]{1,0:T(8,128)(2,1)S(1)}, u32[]{:S(2)}, u32[]{:S(2)}) %collective-permute-start.17) | collective-permute-done | bytes 262176 | tf_op jit(solution)/shard_map/ppermute | solution.py:373
  57.3 2.2 copy-done
  59.4 2.2 copy-done.3
  61.6 2.7 %attend.17 = bf16[128,1152]{1,0:T(8,128)(2,1)S(1)} custom-call(s32[42]{0:T(128)S(1)} %concatenate.6.meta, bf16[128,1024]{1,0:T(8,128)(2,1)S(1)} %collective-permute-done.17.q_ref, bf16[16,256,512]{2,1,0:T(8,128)(2,1)S(1)} %copy-done.3, bf16[16,256,512]{2,1,0:T(8,128)(2,1)S(1)} %copy-done.3, bf16[16,256,512]{2,1,0:T(8,128)(2,1)S(1)} %copy-done.3, ...), custom_call_target="tpu_custom_call" | custom-call | flops 536870912 | bytes 2621440 | tf_op jit(solution)/shard_map/attend/pallas_call | solution.py:207
  64.3 3.2 %collective-permute-start.18 = (bf16[128,1152]{1,0:T(8,128)(2,1)S(1)}, bf16[128,1152]{1,0:T(8,128)(2,1)S(1)}, u32[]{:S(2)}, u32[]{:S(2)}) collective-permute-start(bf16[128,1152]{1,0:T(8,128)(2,1)S(1)} %attend.17), channel_id=1, source_target_pairs={{0,8},{8,16},{16,24},{24,28},{28,20},{20,12},{12,4},{4,0},{1,9},{9... | collective-permute-start | bytes 884744 | tf_op jit(solution)/shard_map/ppermute | solution.py:398
  67.5 5.1 %attend.10 = bf16[128,1152]{1,0:T(8,128)(2,1)S(1)} custom-call(s32[42]{0:T(128)S(1)} %concatenate.6.meta, bf16[128,1024]{1,0:T(8,128)(2,1)S(1)} %collective-permute-done.3.q_ref, bf16[16,256,512]{2,1,0:T(8,128)(2,1)S(1)} %copy-done.3, bf16[16,256,512]{2,1,0:T(8,128)(2,1)S(1)} %copy-done.3, bf16[16,256,512]{2,1,0:T(8,128)(2,1)S(1)} %copy-done.3, ...), custom_call_target="tpu_custom_call" | custom-call | flops 536870912 | bytes 2621440 | tf_op jit(solution)/shard_map/attend/pallas_call | solution.py:207
  72.6 1.1 collective-permute-start.4
  73.7 7.3 %attend.11 = (bf16[128,1152]{1,0:T(8,128)(2,1)S(1)}, bf16[128,1152]{1,0:T(8,128)(2,1)S(1)}) custom-call(s32[42]{0:T(128)S(1)} %concatenate.6.meta, bf16[256,1024]{1,0:T(8,128)(2,1)S(1)} %collective-permute-done.2.q_ref, bf16[16,256,512]{2,1,0:T(8,128)(2,1)S(1)} %copy-done.3, bf16[16,256,512]{2,1,0:T(8,128)(2,1)S(1)} %copy-done.3, ...), custom_call_target="tpu_custom_call" | custom-call | flops 1073741824 | bytes 3145728 | tf_op jit(solution)/shard_map/attend/pallas_call | solution.py:207
  81.0 0.2 collective-permute-start.14
  81.2 9.2 %attend.14 = (bf16[128,1152]{1,0:T(8,128)(2,1)S(1)}, bf16[128,1152]{1,0:T(8,128)(2,1)S(1)}) custom-call(s32[42]{0:T(128)S(1)} %concatenate.6.meta, bf16[256,1024]{1,0:T(8,128)(2,1)S(1)} %collective-permute-done.10.q_ref, bf16[16,256,512]{2,1,0:T(8,128)(2,1)S(1)} %copy-done.3, bf16[16,256,512]{2,1,0:T(8,128)(2,1)S(1)} %copy-done.3, ...), custom_call_target="tpu_custom_call" | custom-call | flops 1073741824 | bytes 3145728 | tf_op jit(solution)/shard_map/attend/pallas_call | solution.py:207
  90.5 0.4 merge.17
  90.9 2.7 %collective-permute-start.19 = (bf16[128,1152]{1,0:T(8,128)(2,1)S(1)}, bf16[128,1152]{1,0:T(8,128)(2,1)S(1)}, u32[]{:S(2)}, u32[]{:S(2)}) collective-permute-start(bf16[128,1152]{1,0:T(8,128)(2,1)S(1)} %merge.17), channel_id=1, source_target_pairs={{0,8},{8,16},{16,24},{24,28},{28,20},{20,12},{12,4},{4,0},{1,9},{9... | collective-permute-start | bytes 884744 | tf_op jit(solution)/shard_map/ppermute | solution.py:403
  93.6 0.4 merge.10
  94.1 4.3 %attend.15 = (bf16[128,1152]{1,0:T(8,128)(2,1)S(1)}, bf16[128,1152]{1,0:T(8,128)(2,1)S(1)}) custom-call(s32[42]{0:T(128)S(1)} %concatenate.6.meta, bf16[256,1024]{1,0:T(8,128)(2,1)S(1)} %collective-permute-done.9.q_ref, bf16[16,256,512]{2,1,0:T(8,128)(2,1)S(1)} %copy-done.3, bf16[16,256,512]{2,1,0:T(8,128)(2,1)S(1)} %copy-done.3, ...), custom_call_target="tpu_custom_call" | custom-call | flops 1073741824 | bytes 3145728 | tf_op jit(solution)/shard_map/attend/pallas_call | solution.py:207
  98.5 9.2 %attend.12 = (bf16[128,1152]{1,0:T(8,128)(2,1)S(1)}, bf16[128,1152]{1,0:T(8,128)(2,1)S(1)}) custom-call(s32[42]{0:T(128)S(1)} %concatenate.6.meta, bf16[256,1024]{1,0:T(8,128)(2,1)S(1)} %copy-done.8, bf16[16,256,512]{2,1,0:T(8,128)(2,1)S(1)} %copy-done.3, bf16[16,256,512]{2,1,0:T(8,128)(2,1)S(1)} %copy-done.3, bf16[16,256,512]{2,1,0:T(8,128)(2,1)S(1)} %copy-done.3, ...), custom_call_target="tpu_custom_call" | custom-call | flops 1073741824 | bytes 3145728 | tf_op jit(solution)/shard_map/attend/pallas_call | solution.py:207
  107.7 0.4 merge.15
  108.1 7.3 %collective-permute-start.15 = (bf16[128,1152]{1,0:T(8,128)(2,1)S(1)}, bf16[128,1152]{1,0:T(8,128)(2,1)S(1)}, u32[]{:S(2)}, u32[]{:S(2)}) collective-permute-start(bf16[128,1152]{1,0:T(8,128)(2,1)S(1)} %merge.15), channel_id=1, source_target_pairs={{8,0},{16,8},{24,16},{28,24},{20,28},{12,20},{4,12},{0,4},{9,1},{1... | collective-permute-start | bytes 884744 | tf_op jit(solution)/shard_map/ppermute | solution.py:405
  115.4 0.4 merge.13
  115.8 3.0 %collective-permute-start.12 = (bf16[128,1152]{1,0:T(8,128)(2,1)S(1)}, bf16[128,1152]{1,0:T(8,128)(2,1)S(1)}, u32[]{:S(2)}, u32[]{:S(2)}) collective-permute-start(bf16[128,1152]{1,0:T(8,128)(2,1)S(1)} %merge.13), channel_id=1, source_target_pairs={{0,8},{8,16},{16,24},{24,28},{28,20},{20,12},{12,4},{4,0},{1,9},{9... | collective-permute-start | bytes 884744 | tf_op jit(solution)/shard_map/ppermute | solution.py:407
  118.8 0.4 merge.18
  119.2 2.1 collective-permute-start.20
  121.2 1.1 merge.11
  122.4 14.6 %copy.46 = bf16[1024,5376]{0,1:T(8,128)(2,1)} copy(bf16[1024,5376]{1,0:T(8,128)(2,1)} %param.10) | data formatting | bytes 22020096 | tf_op args[3]
  137.0 15.2 %copy.47 = bf16[1024,4,1344]{2,0,1:T(8,128)(2,1)} copy(bf16[1024,4,1344]{0,2,1:T(8,128)(2,1)} %bitcast.21) | data formatting | bytes 22020096 | tf_op jit(solution)/shard_map/reshape | solution.py:386
  152.2 2.2 copy-done.1
  154.4 2.2 copy-done.4
  156.6 9.2 %attend.16 = (bf16[128,1152]{1,0:T(8,128)(2,1)S(1)}, bf16[128,1152]{1,0:T(8,128)(2,1)S(1)}) custom-call(s32[42]{0:T(128)S(1)} %concatenate.6.meta, bf16[256,1024]{1,0:T(8,128)(2,1)S(1)} %collective-permute-done.8.q_ref, bf16[16,256,512]{2,1,0:T(8,128)(2,1)S(1)} %copy-done.4, bf16[16,256,512]{2,1,0:T(8,128)(2,1)S(1)} %copy-done.4, ...), custom_call_target="tpu_custom_call" | custom-call | flops 1073741824 | bytes 3145728 | tf_op jit(solution)/shard_map/attend/pallas_call | solution.py:207
  165.8 7.3 %attend.13 = (bf16[128,1152]{1,0:T(8,128)(2,1)S(1)}, bf16[128,1152]{1,0:T(8,128)(2,1)S(1)}) custom-call(s32[42]{0:T(128)S(1)} %concatenate.6.meta, bf16[256,1024]{1,0:T(8,128)(2,1)S(1)} %collective-permute-done.q_ref, bf16[16,256,512]{2,1,0:T(8,128)(2,1)S(1)} %copy-done.4, bf16[16,256,512]{2,1,0:T(8,128)(2,1)S(1)} %copy-done.4, ...), custom_call_target="tpu_custom_call" | custom-call | flops 1073741824 | bytes 3145728 | tf_op jit(solution)/shard_map/attend/pallas_call | solution.py:207
  173.1 0.4 merge.16
  173.6 0.4 merge.14
  174.0 2.1 collective-permute-start.13
  176.1 0.4 merge.19
  176.5 2.0 collective-permute-start.21
  178.4 1.4 merge.12
  179.8 0.4 collective-permute-start.7
  180.2 9.0 %attend.9 = (bf16[128,1152]{1,0:T(8,128)(2,1)S(1)}, bf16[128,1152]{1,0:T(8,128)(2,1)S(1)}) custom-call(s32[42]{0:T(128)S(1)} %concatenate.6.meta, bf16[256,1024]{1,0:T(8,128)(2,1)S(1)} %copy-done.6, bf16[16,256,512]{2,1,0:T(8,128)(2,1)S(1)} %copy-done.5, bf16[16,256,512]{2,1,0:T(8,128)(2,1)S(1)} %copy-done.5, bf16[16,256,512]{2,1,0:T(8,128)(2,1)S(1)} %copy-done.5, ...), custom_call_target="tpu_custom_call" | custom-call | flops 1073741824 | bytes 3145728 | tf_op jit(solution)/shard_map/attend/pallas_call | solution.py:207
  189.4 9.4 %finish.1 = (bf16[2,256,1344]{2,1,0:T(8,128)(2,1)S(1)}, bf16[2,256,1344]{2,1,0:T(8,128)(2,1)S(1)}) custom-call(s32[42]{0:T(128)S(1)} %concatenate.6.meta, s32[4]{0:T(128)S(1)} %pad_add_fusion.target, bf16[128,1152]{1,0:T(8,128)(2,1)S(1)} %get-tuple-element.21.refs_0_, bf16[128,1152]{1,0:T(8,128)(2,1)S(1)} %collective-permute-done.7.refs_1_, ...), custom_call_target="tpu_custom_call" | custom-call | flops 2818572288 | bytes 11010048 | tf_op jit(solution)/shard_map/finish/pallas_call | solution.py:324
  198.8 1.6 copy.48
  200.4 3.5 %collective-permute-done.22 = bf16[2,256,1344]{1,2,0:T(8,128)(2,1)} collective-permute-done((bf16[2,256,1344]{1,2,0:T(8,128)(2,1)}, bf16[2,256,1344]{1,2,0:T(8,128)(2,1)}, u32[]{:S(2)}, u32[]{:S(2)}) %collective-permute-start.22) | collective-permute-done | bytes 1376288 | tf_op jit(solution)/shard_map/ppermute | solution.py:417
  203.8 1.8 copy.49
  205.6 0.3 convert_add_fusion
  205.9 1.5 copy-done.9
  207.5 0.9 fusion.2
  208.4 2.4 %copy.50 = bf16[256,1344]{0,1:T(8,128)(2,1)} copy(bf16[256,1344]{1,0:T(8,128)(2,1)} %fusion.2) | data formatting | bytes 1376256 | tf_op jit(solution)/shard_map/convert_element_type | solution.py:422
  210.8 1.5 collective-permute-start.23
  212.3 16.3 %collective-permute-done.23 = bf16[256,1344]{0,1:T(8,128)(2,1)} collective-permute-done((bf16[256,1344]{0,1:T(8,128)(2,1)}, bf16[256,1344]{0,1:T(8,128)(2,1)}, u32[]{:S(2)}, u32[]{:S(2)}) %collective-permute-start.23) | collective-permute-done | bytes 688160 | tf_op jit(solution)/shard_map/ppermute | solution.py:422
  228.6 2.5 %copy.51 = f32[256,1344]{1,0:T(8,128)} copy(bf16[256,1344]{0,1:T(8,128)(2,1)} %collective-permute-done.23) | data formatting | bytes 2064384 | tf_op jit(solution)/shard_map/convert_element_type | solution.py:422
  231.0 2.3 fusion.1
  233.4 2.2 copy.52
  (60 shorter events, 1.1 us)
Async XLA Ops:
  0.0 24.1 %collective-permute-start.8 = (bf16[256,1024]{1,0:T(8,128)(2,1)}, bf16[256,1024]{1,0:T(8,128)(2,1)S(1)}, u32[]{:S(2)}, u32[]{:S(2)}) collective-permute-start(bf16[256,1024]{1,0:T(8,128)(2,1)} %q_ref.1), channel_id=1, source_target_pairs={{8,0},{16,8},{24,16},{28,24},{20,28},{12,20},{4,12},{0,4},{9,1},{1... | collective-permute-start | bytes 1572872 | tf_op jit(solution)/shard_map/ppermute | solution.py:371
  2.9 23.1 %collective-permute-start = (bf16[256,1024]{1,0:T(8,128)(2,1)}, bf16[256,1024]{1,0:T(8,128)(2,1)S(1)}, u32[]{:S(2)}, u32[]{:S(2)}) collective-permute-start(bf16[256,1024]{1,0:T(8,128)(2,1)} %q_ref.1), channel_id=1, source_target_pairs={{0,8},{8,16},{16,24},{24,28},{28,20},{20,12},{12,4},{4,0},{1,9},{9... | collective-permute-start | bytes 1572872 | tf_op jit(solution)/shard_map/ppermute | solution.py:370
  19.3 6.8 %copy-start.11 = (s32[4,32]{1,0:T(4,128)S(1)}, s32[4,32]{1,0:T(4,128)}, u32[]{:S(2)}) copy-start(s32[4,32]{1,0:T(4,128)} %param.11) | copy-start | bytes 1540
  19.3 32.8 %copy-start.12 = (s32[4]{0:T(128)S(1)}, s32[4]{0:T(128)}, u32[]{:S(2)}) copy-start(s32[4]{0:T(128)} %param.12) | copy-start | bytes 52
  19.3 33.1 %copy-start.13 = (s32[4]{0:T(128)S(1)}, s32[4]{0:T(128)}, u32[]{:S(2)}) copy-start(s32[4]{0:T(128)} %param.13) | copy-start | bytes 52
  24.1 13.4 %collective-permute-start.9 = (bf16[256,1024]{1,0:T(8,128)(2,1)S(1)}, bf16[256,1024]{1,0:T(8,128)(2,1)S(1)}, u32[]{:S(2)}, u32[]{:S(2)}) collective-permute-start(bf16[256,1024]{1,0:T(8,128)(2,1)S(1)} %collective-permute-done.8.q_ref), channel_id=1, source_target_pairs={{8,0},{16,8},{24,16},{28,24},{20,28},{12,20},{4,12},{0,4},{9,1},{1... | collective-permute-start | bytes 1572872 | tf_op jit(solution)/shard_map/ppermute | solution.py:371
  26.1 13.2 %collective-permute-start.1 = (bf16[256,1024]{1,0:T(8,128)(2,1)S(1)}, bf16[256,1024]{1,0:T(8,128)(2,1)S(1)}, u32[]{:S(2)}, u32[]{:S(2)}) collective-permute-start(bf16[256,1024]{1,0:T(8,128)(2,1)S(1)} %collective-permute-done.q_ref), channel_id=1, source_target_pairs={{0,8},{8,16},{16,24},{24,28},{28,20},{20,12},{12,4},{4,0},{1,9},{9... | collective-permute-start | bytes 1572872 | tf_op jit(solution)/shard_map/ppermute | solution.py:370
  37.5 12.5 %collective-permute-start.10 = (bf16[256,1024]{1,0:T(8,128)(2,1)S(1)}, bf16[256,1024]{1,0:T(8,128)(2,1)S(1)}, u32[]{:S(2)}, u32[]{:S(2)}) collective-permute-start(bf16[256,1024]{1,0:T(8,128)(2,1)S(1)} %collective-permute-done.9.q_ref), channel_id=1, source_target_pairs={{8,0},{16,8},{24,16},{28,24},{20,28},{12,20},{4,12},{0,4},{9,1},{1... | collective-permute-start | bytes 1572872 | tf_op jit(solution)/shard_map/ppermute | solution.py:371
  39.3 13.9 %copy-start.7 = (bf16[256,1024]{1,0:T(8,128)(2,1)}, bf16[256,1024]{1,0:T(8,128)(2,1)S(1)}, u32[]{:S(2)}) copy-start(bf16[256,1024]{1,0:T(8,128)(2,1)S(1)} %collective-permute-done.1.q_ref) | copy-start | bytes 1572868
  39.3 13.2 %collective-permute-start.2 = (bf16[256,1024]{1,0:T(8,128)(2,1)S(1)}, bf16[256,1024]{1,0:T(8,128)(2,1)S(1)}, u32[]{:S(2)}, u32[]{:S(2)}) collective-permute-start(bf16[256,1024]{1,0:T(8,128)(2,1)S(1)} %collective-permute-done.1.q_ref), channel_id=1, source_target_pairs={{0,8},{8,16},{16,24},{24,28},{28,20},{20,12},{12,4},{4,0},{1,9},{9... | collective-permute-start | bytes 1572872 | tf_op jit(solution)/shard_map/ppermute | solution.py:370
  50.7 6.6 %collective-permute-start.17 = (bf16[128,1024]{1,0:T(8,128)(2,1)}, bf16[128,1024]{1,0:T(8,128)(2,1)S(1)}, u32[]{:S(2)}, u32[]{:S(2)}) collective-permute-start(bf16[128,1024]{1,0:T(8,128)(2,1)} %slice.34), channel_id=1, source_target_pairs={{8,0},{16,8},{24,16},{28,24},{20,28},{12,20},{4,12},{0,4},{9,1},{1... | collective-permute-start | bytes 786440 | tf_op jit(solution)/shard_map/ppermute | solution.py:373
  52.5 14.9 %collective-permute-start.3 = (bf16[128,1024]{1,0:T(8,128)(2,1)S(1)}, bf16[128,1024]{1,0:T(8,128)(2,1)S(1)}, u32[]{:S(2)}, u32[]{:S(2)}) collective-permute-start(bf16[128,1024]{1,0:T(8,128)(2,1)S(1)} %slice.33), channel_id=1, source_target_pairs={{0,8},{8,16},{16,24},{24,28},{28,20},{20,12},{12,4},{4,0},{1,9},{9... | collective-permute-start | bytes 786440 | tf_op jit(solution)/shard_map/ppermute | solution.py:372
  57.3 2.2 copy-start
  59.4 2.2 copy-start.3
  64.3 26.2 %collective-permute-start.18 = (bf16[128,1152]{1,0:T(8,128)(2,1)S(1)}, bf16[128,1152]{1,0:T(8,128)(2,1)S(1)}, u32[]{:S(2)}, u32[]{:S(2)}) collective-permute-start(bf16[128,1152]{1,0:T(8,128)(2,1)S(1)} %attend.17), channel_id=1, source_target_pairs={{0,8},{8,16},{16,24},{24,28},{28,20},{20,12},{12,4},{4,0},{1,9},{9... | collective-permute-start | bytes 884744 | tf_op jit(solution)/shard_map/ppermute | solution.py:398
  72.6 21.1 %collective-permute-start.4 = (bf16[128,1152]{1,0:T(8,128)(2,1)S(1)}, bf16[128,1152]{1,0:T(8,128)(2,1)S(1)}, u32[]{:S(2)}, u32[]{:S(2)}) collective-permute-start(bf16[128,1152]{1,0:T(8,128)(2,1)S(1)} %attend.10), channel_id=1, source_target_pairs={{8,0},{16,8},{24,16},{28,24},{20,28},{12,20},{4,12},{0,4},{9,1},{1... | collective-permute-start | bytes 884744 | tf_op jit(solution)/shard_map/ppermute | solution.py:397
  81.0 26.7 %collective-permute-start.14 = (bf16[128,1152]{1,0:T(8,128)(2,1)S(1)}, bf16[128,1152]{1,0:T(8,128)(2,1)S(1)}, u32[]{:S(2)}, u32[]{:S(2)}) collective-permute-start(bf16[128,1152]{1,0:T(8,128)(2,1)S(1)} %get-tuple-element.29), channel_id=1, source_target_pairs={{8,0},{16,8},{24,16},{28,24},{20,28},{12,20},{4,12},{0,4},{9,1},{1... | collective-permute-start | bytes 884744 | tf_op jit(solution)/shard_map/ppermute | solution.py:405
  90.4 24.9 %collective-permute-start.11 = (bf16[128,1152]{1,0:T(8,128)(2,1)S(1)}, bf16[128,1152]{1,0:T(8,128)(2,1)S(1)}, u32[]{:S(2)}, u32[]{:S(2)}) collective-permute-start(bf16[128,1152]{1,0:T(8,128)(2,1)S(1)} %get-tuple-element.25), channel_id=1, source_target_pairs={{0,8},{8,16},{16,24},{24,28},{28,20},{20,12},{12,4},{4,0},{1,9},{9... | collective-permute-start | bytes 884744 | tf_op jit(solution)/shard_map/ppermute | solution.py:407
  90.9 27.9 %collective-permute-start.19 = (bf16[128,1152]{1,0:T(8,128)(2,1)S(1)}, bf16[128,1152]{1,0:T(8,128)(2,1)S(1)}, u32[]{:S(2)}, u32[]{:S(2)}) collective-permute-start(bf16[128,1152]{1,0:T(8,128)(2,1)S(1)} %merge.17), channel_id=1, source_target_pairs={{0,8},{8,16},{16,24},{24,28},{28,20},{20,12},{12,4},{4,0},{1,9},{9... | collective-permute-start | bytes 884744 | tf_op jit(solution)/shard_map/ppermute | solution.py:403
  94.0 4.4 %copy-start.8 = (bf16[256,1024]{1,0:T(8,128)(2,1)S(1)}, bf16[256,1024]{1,0:T(8,128)(2,1)}, u32[]{:S(2)}) copy-start(bf16[256,1024]{1,0:T(8,128)(2,1)} %copy-done.7) | copy-start | bytes 1572868
  94.0 27.2 %collective-permute-start.5 = (bf16[128,1152]{1,0:T(8,128)(2,1)S(1)}, bf16[128,1152]{1,0:T(8,128)(2,1)S(1)}, u32[]{:S(2)}, u32[]{:S(2)}) collective-permute-start(bf16[128,1152]{1,0:T(8,128)(2,1)S(1)} %merge.10), channel_id=1, source_target_pairs={{8,0},{16,8},{24,16},{28,24},{20,28},{12,20},{4,12},{0,4},{9,1},{1... | collective-permute-start | bytes 884744 | tf_op jit(solution)/shard_map/ppermute | solution.py:402
  108.1 65.0 %collective-permute-start.15 = (bf16[128,1152]{1,0:T(8,128)(2,1)S(1)}, bf16[128,1152]{1,0:T(8,128)(2,1)S(1)}, u32[]{:S(2)}, u32[]{:S(2)}) collective-permute-start(bf16[128,1152]{1,0:T(8,128)(2,1)S(1)} %merge.15), channel_id=1, source_target_pairs={{8,0},{16,8},{24,16},{28,24},{20,28},{12,20},{4,12},{0,4},{9,1},{1... | collective-permute-start | bytes 884744 | tf_op jit(solution)/shard_map/ppermute | solution.py:405
  115.8 57.8 %collective-permute-start.12 = (bf16[128,1152]{1,0:T(8,128)(2,1)S(1)}, bf16[128,1152]{1,0:T(8,128)(2,1)S(1)}, u32[]{:S(2)}, u32[]{:S(2)}) collective-permute-start(bf16[128,1152]{1,0:T(8,128)(2,1)S(1)} %merge.13), channel_id=1, source_target_pairs={{0,8},{8,16},{16,24},{24,28},{28,20},{20,12},{12,4},{4,0},{1,9},{9... | collective-permute-start | bytes 884744 | tf_op jit(solution)/shard_map/ppermute | solution.py:407
  119.2 56.9 %collective-permute-start.20 = (bf16[128,1152]{1,0:T(8,128)(2,1)S(1)}, bf16[128,1152]{1,0:T(8,128)(2,1)S(1)}, u32[]{:S(2)}, u32[]{:S(2)}) collective-permute-start(bf16[128,1152]{1,0:T(8,128)(2,1)S(1)} %merge.18), channel_id=1, source_target_pairs={{0,8},{8,16},{16,24},{24,28},{28,20},{20,12},{12,4},{4,0},{1,9},{9... | collective-permute-start | bytes 884744 | tf_op jit(solution)/shard_map/ppermute | solution.py:403
  122.4 56.1 %collective-permute-start.6 = (bf16[128,1152]{1,0:T(8,128)(2,1)}, bf16[128,1152]{1,0:T(8,128)(2,1)}, u32[]{:S(2)}, u32[]{:S(2)}) collective-permute-start(bf16[128,1152]{1,0:T(8,128)(2,1)} %merge.11), channel_id=1, source_target_pairs={{8,0},{16,8},{24,16},{28,24},{20,28},{12,20},{4,12},{0,4},{9,1},{1... | collective-permute-start | bytes 884744 | tf_op jit(solution)/shard_map/ppermute | solution.py:402
  152.2 2.2 copy-start.1
  154.4 2.2 copy-start.4
  165.8 14.5 %copy-start.2 = (bf16[16,256,512]{2,1,0:T(8,128)(2,1)S(1)}, bf16[16,256,512]{2,1,0:T(8,128)(2,1)}, u32[]{:S(2)}) copy-start(bf16[16,256,512]{2,1,0:T(8,128)(2,1)} %get-tuple-element.47.refs_4_.refs_5_.refs_6_.refs_7_) | copy-start | bytes 12582916
  165.8 14.5 %copy-start.5 = (bf16[16,256,512]{2,1,0:T(8,128)(2,1)S(1)}, bf16[16,256,512]{2,1,0:T(8,128)(2,1)}, u32[]{:S(2)}) copy-start(bf16[16,256,512]{2,1,0:T(8,128)(2,1)} %get-tuple-element.48.refs_0_.refs_1_.refs_2_.refs_3_) | copy-start | bytes 12582916
  173.1 7.2 %copy-start.6 = (bf16[256,1024]{1,0:T(8,128)(2,1)S(1)}, bf16[256,1024]{1,0:T(8,128)(2,1)}, u32[]{:S(2)}) copy-start(bf16[256,1024]{1,0:T(8,128)(2,1)} %q_ref.1) | copy-start | bytes 1572868
  173.5 15.9 %collective-permute-start.16 = (bf16[128,1152]{1,0:T(8,128)(2,1)S(1)}, bf16[128,1152]{1,0:T(8,128)(2,1)S(1)}, u32[]{:S(2)}, u32[]{:S(2)}) collective-permute-start(bf16[128,1152]{1,0:T(8,128)(2,1)S(1)} %merge.16), channel_id=1, source_target_pairs={{8,0},{16,8},{24,16},{28,24},{20,28},{12,20},{4,12},{0,4},{9,1},{1... | collective-permute-start | bytes 884744 | tf_op jit(solution)/shard_map/ppermute | solution.py:405
  174.0 15.4 %collective-permute-start.13 = (bf16[128,1152]{1,0:T(8,128)(2,1)S(1)}, bf16[128,1152]{1,0:T(8,128)(2,1)S(1)}, u32[]{:S(2)}, u32[]{:S(2)}) collective-permute-start(bf16[128,1152]{1,0:T(8,128)(2,1)S(1)} %merge.14), channel_id=1, source_target_pairs={{0,8},{8,16},{16,24},{24,28},{28,20},{20,12},{12,4},{4,0},{1,9},{9... | collective-permute-start | bytes 884744 | tf_op jit(solution)/shard_map/ppermute | solution.py:407
  176.5 12.9 %collective-permute-start.21 = (bf16[128,1152]{1,0:T(8,128)(2,1)S(1)}, bf16[128,1152]{1,0:T(8,128)(2,1)S(1)}, u32[]{:S(2)}, u32[]{:S(2)}) collective-permute-start(bf16[128,1152]{1,0:T(8,128)(2,1)S(1)} %merge.19), channel_id=1, source_target_pairs={{0,8},{8,16},{16,24},{24,28},{28,20},{20,12},{12,4},{4,0},{1,9},{9... | collective-permute-start | bytes 884744 | tf_op jit(solution)/shard_map/ppermute | solution.py:403
  179.8 9.6 %collective-permute-start.7 = (bf16[128,1152]{1,0:T(8,128)(2,1)S(1)}, bf16[128,1152]{1,0:T(8,128)(2,1)S(1)}, u32[]{:S(2)}, u32[]{:S(2)}) collective-permute-start(bf16[128,1152]{1,0:T(8,128)(2,1)S(1)} %merge.12), channel_id=1, source_target_pairs={{8,0},{16,8},{24,16},{28,24},{20,28},{12,20},{4,12},{0,4},{9,1},{1... | collective-permute-start | bytes 884744 | tf_op jit(solution)/shard_map/ppermute | solution.py:402
  200.3 3.5 %collective-permute-start.22 = (bf16[2,256,1344]{1,2,0:T(8,128)(2,1)}, bf16[2,256,1344]{1,2,0:T(8,128)(2,1)}, u32[]{:S(2)}, u32[]{:S(2)}) collective-permute-start(bf16[2,256,1344]{1,2,0:T(8,128)(2,1)} %copy.48), channel_id=1, source_target_pairs={{0,1},{1,0},{2,3},{3,2},{4,5},{5,4},{6,7},{7,6},{8,9},{9,8},{10,11... | collective-permute-start | bytes 4128776 | tf_op jit(solution)/shard_map/ppermute | solution.py:417
  205.9 1.6 copy-start.9
  208.4 22.6 %copy-start.10 = (f32[2,256,1344]{2,1,0:T(8,128)S(1)}, f32[2,256,1344]{2,1,0:T(8,128)}, u32[]{:S(2)}) copy-start(f32[2,256,1344]{2,1,0:T(8,128)} %copy-done.9) | copy-start | bytes 8257540
  210.8 17.8 %collective-permute-start.23 = (bf16[256,1344]{0,1:T(8,128)(2,1)}, bf16[256,1344]{0,1:T(8,128)(2,1)}, u32[]{:S(2)}, u32[]{:S(2)}) collective-permute-start(bf16[256,1344]{0,1:T(8,128)(2,1)} %copy.50), channel_id=1, source_target_pairs={{0,2},{1,3},{2,0},{3,1},{4,6},{5,7},{6,4},{7,5},{8,10},{9,11},{10,... | collective-permute-start | bytes 2064392 | tf_op jit(solution)/shard_map/ppermute | solution.py:422
